TPU v7x, 128 devices: a whole 4x4x4 slice. The times are simulated.
128 devices in a mesh: dp: 16 (over y_hi, x, core), space: 8 (over z, y_lo).
Axes of the slice: x: 4, y: 4 (y_hi: 2, y_lo: 2; y = y_hi * 2 + y_lo), z: 4, core: 2. Of those that a mesh axis runs over, the one named last changes fastest.
Arguments:
- volume: bfloat16 [16, 32, 32, 128], P('dp', 'space'), may hold values from -6 to 6
- first_kernel: bfloat16 [3, 3, 3, 4, 64], replicated, may hold values from -0.625 to 0.625
- mid_kernel: bfloat16 [3, 3, 3, 64, 128], replicated, may hold values from -0.15625 to 0.15625
- deep_kernel: bfloat16 [3, 3, 3, 128, 256], replicated, may hold values from -0.109375 to 0.109375
- deep_cotangent: bfloat16 [16, 16, 16, 16, 256], P('dp', 'space'), may hold values from -6 to 6
Outputs:
- deep_output: bfloat16 [16, 16, 16, 16, 256], P('dp', 'space')
- deep_kernel_grad: float32 [3, 3, 3, 128, 256], P(None, None, None, 'space')
- mid_kernel_grad: float32 [3, 3, 3, 64, 128], replicated
All inputs are finite; a program needn't handle non-finite values.
Results may differ from a plain program's by a relative error of at most 0.024.
Values may be sent and summed in bfloat16 or wider, within the bound.
A program may use at most 128 MiB of HBM per device.

v0:
```python
import math
import jax
import jax.numpy as jnp
from jax import lax
from jax.sharding import PartitionSpec as P

SLOPE = 0.3


def padded_2(block, sides, width):
    for axis, dim in sides:
        count = lax.axis_size(axis)
        forward = [(i, i + 1) for i in range(count - 1)]
        backward = [(target, source) for source, target in forward]
        low = lax.ppermute(
            lax.slice_in_dim(block, block.shape[dim] - width, None, axis=dim), axis, forward
        )
        high = lax.ppermute(lax.slice_in_dim(block, 0, width, axis=dim), axis, backward)
        block = jnp.concatenate([low, block, high], axis=dim)
    return block


def activate(value):
    return SLOPE * value + (1.0 - SLOPE) * value * jax.nn.sigmoid(value)


def activate_slope(value):
    sig = jax.nn.sigmoid(value)
    return SLOPE + (1.0 - SLOPE) * (sig + value * sig * (1.0 - sig))


def conv_depth(padded, kernel):
    return lax.conv_general_dilated(
        padded[None],
        kernel,
        (1, 1, 1),
        [(0, 0), (1, 1), (1, 1)],
        dimension_numbers=("NDHWC", "DHWIO", "NDHWC"),
        preferred_element_type=jnp.float32,
    )[0]


def pool_cells(values):
    dd, hh, ww, cc = values.shape
    return values.reshape(dd // 2, 2, hh // 2, 2, ww // 2, 2, cc).mean(axis=(1, 3, 5))


def expand(values):
    return jnp.repeat(jnp.repeat(jnp.repeat(values, 2, 0), 2, 1), 2, 2)


def kernel_grad(padded, cotangent):
    dd, hh, ww, _ = cotangent.shape
    tap_list = []
    for depth_off in range(3):
        for row_off in range(3):
            for col_off in range(3):
                window = padded[
                    depth_off : depth_off + dd, row_off : row_off + hh, col_off : col_off + ww
                ]
                tap_list.append(
                    jnp.einsum(
                        "dhwi,dhwo->io", window, cotangent, preferred_element_type=jnp.float32
                    )
                )
    return jnp.stack(tap_list).reshape(3, 3, 3, padded.shape[-1], cotangent.shape[-1])


def pad_sides(values):
    return jnp.pad(values, ((0, 0), (1, 1), (1, 1), (0, 0)))


def pad_depth(values):
    return jnp.pad(values, ((1, 1), (0, 0), (0, 0), (0, 0)))


def pad_cells(values):
    return jnp.pad(values, ((1, 1), (1, 1), (1, 1), (0, 0)))


def on_device(volume, first_kernel, mid_kernel, deep_kernel, deep_cotangent):
    slab_depth = volume.shape[1]
    side_cells = volume.shape[2]
    in_channels = volume.shape[3] // side_cells
    space_count = lax.axis_size("space")
    space_index = lax.axis_index("space")
    input_field = volume[0].reshape(slab_depth, side_cells, side_cells, in_channels)
    padded = padded_2(input_field, (("space", 0),), 1)
    own_hidden = activate(conv_depth(padded, first_kernel)).astype(jnp.bfloat16)
    hidden = padded_2(own_hidden, (("space", 0),), 1)
    pre_mid = conv_depth(hidden, mid_kernel)
    pooled = pool_cells(activate(pre_mid)).astype(jnp.bfloat16)
    cotangent = deep_cotangent[0].astype(jnp.float32)
    columns = lax.all_to_all(pooled, "space", split_axis=3, concat_axis=0, tiled=True)
    chan_width = columns.shape[3]
    chan_start = space_index * chan_width
    kernel_part = lax.dynamic_slice_in_dim(deep_kernel, chan_start, chan_width, 3)
    partial_value = conv_depth(pad_depth(columns), kernel_part)
    pre_deep = lax.psum_scatter(partial_value, "space", scatter_dimension=0, tiled=True)
    grad_pre = (cotangent * activate_slope(pre_deep)).astype(jnp.bfloat16)
    all_cotangent = lax.all_gather(grad_pre, "space", axis=0, tiled=True)
    deep_grad = kernel_grad(pad_cells(columns), all_cotangent)
    flipped_part = jnp.swapaxes(kernel_part[::-1, ::-1, ::-1], 3, 4)
    back_grad = conv_depth(pad_depth(all_cotangent), flipped_part).astype(jnp.bfloat16)
    pooled_grad = lax.all_to_all(back_grad, "space", split_axis=0, concat_axis=3, tiled=True)
    deep_grad = lax.psum(deep_grad.astype(jnp.bfloat16), "dp").astype(jnp.float32)
    grad_mid = (expand(pooled_grad.astype(jnp.float32)) * 0.125 * activate_slope(pre_mid)).astype(
        jnp.bfloat16
    )
    mid_grad = lax.psum(kernel_grad(pad_sides(hidden), grad_mid), ("dp", "space"))
    device_total = lax.axis_size("dp") * space_count
    cell_count = slab_depth * side_cells * side_cells
    deep_scale = math.sqrt(device_total * cell_count // 8)
    mid_scale = math.sqrt(device_total * cell_count)
    deep_output = activate(pre_deep).astype(jnp.bfloat16)[None]
    return (deep_output, deep_grad / deep_scale, mid_grad / mid_scale)


def solution(mesh):
    in_specs = (P("dp", "space", None, None), P(), P(), P(), P("dp", "space", None, None, None))
    out_specs = (P("dp", "space", None, None, None), P(None, None, None, "space", None), P())
    return jax.shard_map(
        on_device, mesh=mesh, in_specs=in_specs, out_specs=out_specs, check_vma=False
    )
```

profile of v0, /device:TPU:1, one launch (start us, length us, event | category | flops | bytes accessed | tf_op | source)
XLA Modules:
  0.0 628.2 jit_solution(16983838333227108347)
XLA Ops:
  8.2 4.0 collective-permute-start
  13.6 3.4 collective-permute-done.1
  18.2 7.4 %add_convert_fusion = (bf16[4,32,8,5,64]{4,2,3,1,0:T(8,128)(2,1)}, f32[4,32,8,5,64]{4,2,3,1,0:T(8,128)S(1)}, f32[4,32,8,5,64]{4,2,3,1,0:T(8,128)S(1)}, f32[4,32,8,5,64]{4,2,3,1,0:T(8,128)S(1)}) fusion(pred[8,5]{0,1:T(8,128)(4,1)S(1)} %copy-done.21, bf16[3,3,3,4,64]{4,3,2,1,0:T(4,128)(2,1)S(1)} %copy-done.20, bf16[6,32,1,7,2,4]{3,5,4,1,0,2:T(4,128)(2,1)S(1)} %slice.257, ...), kind=kOutput, calls=%fused_computation.31 | convolution fusion | flops 72511488 | bytes 4684328 | tf_op jit(solution)/shard_map/conv_general_dilated | solution.py:33
  27.5 4.8 fusion.30
  32.4 4.3 collective-permute-start.2
  40.0 7.1 %collective-permute-done.3 = bf16[1,32,32,64]{3,2,1,0:T(8,128)(2,1)S(1)} collective-permute-done((bf16[1,32,32,64]{3,2,1,0:T(8,128)(2,1)S(1)}, bf16[1,32,32,64]{3,2,1,0:T(8,128)(2,1)S(1)}, u32[]{:S(2)}, u32[]{:S(2)}) %collective-permute-start.3) | collective-permute-done | bytes 131104 | tf_op jit(solution)/shard_map/ppermute | solution.py:18
  50.6 6.6 %broadcast_multiply_fusion.1 = (f32[4,32,8,5,128]{4,2,3,1,0:T(8,128)S(1)}, f32[4,32,8,5,128]{4,2,3,1,0:T(8,128)S(1)}, f32[4,32,8,5,128]{4,2,3,1,0:T(8,128)S(1)}, f32[4,32,8,5,128]{4,2,3,1,0:T(8,128)}) fusion(bf16[3,3,3,64,128]{4,3,2,1,0:T(8,128)(2,1)S(1)} %copy-done.19, bf16[6,32,1,7,2,64]{5,3,4,1,0,2:T(8,128)(2,1)S(1)} %slice.263, ...), kind=kOutput, calls=%fused_computation.97 | convolution fusion | flops 2225799168 | bytes 12255272 | tf_op jit(solution)/shard_map/conv_general_dilated | solution.py:33
  60.7 2.9 reduce_sum.9
  67.0 5.2 all-to-all-start
  72.3 5.5 all-to-all-done
  82.5 4.0 copy.321
  86.4 2.8 pad.24.clone
  89.3 5.7 copy.215
  96.8 4.5 broadcast_select_fusion
  106.2 93.6 %reduce-scatter.2.cloned.1.call-done = f32[2,16,16,256]{3,1,2,0:T(8,128)} async-done(((f32[16,16,16,256]{3,1,2,0:T(8,128)}), f32[2,16,16,256]{3,1,2,0:T(8,128)}) %reduce-scatter.2.cloned.1.call-update) | async-done | bytes 524304 | tf_op jit(solution)/shard_map/reduce_scatter | solution.py:99
  208.3 46.0 %all-gather.2.cloned.1.call-done = bf16[16,16,16,256]{3,2,1,0:T(8,128)(2,1)} async-done(((bf16[2,16,16,256]{3,2,1,0:T(8,128)(2,1)}), bf16[16,16,16,256]{3,2,1,0:T(8,128)(2,1)}) %all-gather.2.cloned.1.call-update) | async-done | bytes 2097168 | tf_op jit(solution)/shard_map/all_gather | solution.py:101
  259.6 22.7 %select_convert_fusion = bf16[16,16,8,3,16]{4,2,3,1,0:T(8,128)(2,1)S(1)} fusion(pred[8,3]{0,1:T(4,128)(4,1)S(1)} %copy-done.22, bf16[18,16,1,7,2,256]{5,3,4,1,0,2:T(8,128)(2,1)S(1)} %slice.269, bf16[18,16,1,8,3,256]{5,3,4,1,0,2:T(8,128)(2,1)S(1)} %copy.221, bf16[3,3,3,128,256]{4,3,2,1,0:T(8,128)(2,1)S(1)} %copy-done, s32[]{:T(128)S(6)} %select_n.3), kind=kOutput, calls=%fused_computation.13 | convolution fusion | flops 1320222720 | bytes 6316548 | tf_op jit(solution)/shard_map/conv_general_dilated | solution.py:33
  283.9 3.1 reshape.225
  287.0 3.4 all-to-all-start.1
  290.6 3.0 fusion.179
  293.5 2.9 fusion.177
  332.1 2.6 copy.314
  365.0 101.8 %all-reduce.7.cloned.1.call-done = bf16[3,3,3,16,256]{4,3,2,1,0:T(8,128)(2,1)} async-done(((bf16[3,3,3,16,256]{4,3,2,1,0:T(8,128)(2,1)}), bf16[3,3,3,16,256]{4,3,2,1,0:T(8,128)(2,1)}) %all-reduce.7.cloned.1.call-update) | async-done | bytes 221200 | tf_op jit(solution)/shard_map/psum | solution.py:106
  468.6 150.7 %all-reduce.9.cloned.1.call-done = f32[3,3,3,64,128]{4,3,2,1,0:T(8,128)} async-done(((f32[3,3,3,64,128]{4,3,2,1,0:T(8,128)}), f32[3,3,3,64,128]{4,3,2,1,0:T(8,128)}) %all-reduce.9.cloned.1.call-update) | async-done | bytes 884752 | tf_op jit(solution)/shard_map/psum | solution.py:110
  (167 shorter events, 115.6 us)
Async XLA Ops:
  7.2 89.5 %copy-start = (bf16[3,3,3,128,256]{4,3,2,1,0:T(8,128)(2,1)S(1)}, bf16[3,3,3,128,256]{4,3,2,1,0:T(8,128)(2,1)}, u32[]{:S(2)}) copy-start(bf16[3,3,3,128,256]{4,3,2,1,0:T(8,128)(2,1)} %param.8) | copy-start | bytes 5308420
  7.2 11.0 %copy-start.21 = (pred[8,5]{0,1:T(8,128)(4,1)S(1)}, pred[8,5]{0,1:T(8,128)(4,1)}, u32[]{:S(2)}) copy-start(pred[8,5]{0,1:T(8,128)(4,1)} %constant.63) | copy-start | bytes 124
  7.2 11.0 %copy-start.20 = (bf16[3,3,3,4,64]{4,3,2,1,0:T(4,128)(2,1)S(1)}, bf16[3,3,3,4,64]{4,3,2,1,0:T(4,128)(2,1)}, u32[]{:S(2)}) copy-start(bf16[3,3,3,4,64]{4,3,2,1,0:T(4,128)(2,1)} %param.6) | copy-start | bytes 41476
  8.2 5.3 collective-permute-start
  12.3 4.7 collective-permute-start.1
  32.3 16.2 %copy-start.6 = (bf16[4,32,1,32,64]{4,3,1,2,0:T(8,128)(2,1)}, bf16[4,32,1,32,64]{4,3,1,2,0:T(8,128)(2,1)S(1)}, u32[]{:S(2)}) copy-start(bf16[4,32,1,32,64]{4,3,1,2,0:T(8,128)(2,1)S(1)} %fusion.30) | copy-start | bytes 1572868
  32.4 7.6 %collective-permute-start.2 = (bf16[1,32,32,64]{3,2,1,0:T(8,128)(2,1)S(1)}, bf16[1,32,32,64]{3,2,1,0:T(8,128)(2,1)S(1)}, u32[]{:S(2)}, u32[]{:S(2)}) collective-permute-start(bf16[1,32,32,64]{3,2,1,0:T(8,128)(2,1)S(1)} %get-tuple-element.18), channel_id=1, source_target_pairs={{0,1},{1,2},{2,3},{3,4},{4,5},{5,6},{6,7},{8,9},{9,10},{10,11},{11... | collective-permute-start | bytes 393224 | tf_op jit(solution)/shard_map/ppermute | solution.py:15
  36.7 10.3 %collective-permute-start.3 = (bf16[1,32,32,64]{3,2,1,0:T(8,128)(2,1)S(1)}, bf16[1,32,32,64]{3,2,1,0:T(8,128)(2,1)S(1)}, u32[]{:S(2)}, u32[]{:S(2)}) collective-permute-start(bf16[1,32,32,64]{3,2,1,0:T(8,128)(2,1)S(1)} %get-tuple-element.19), channel_id=1, source_target_pairs={{1,0},{2,1},{3,2},{4,3},{5,4},{6,5},{7,6},{9,8},{10,9},{11,10},{12... | collective-permute-start | bytes 393224 | tf_op jit(solution)/shard_map/ppermute | solution.py:18
  40.0 8.6 %copy-start.16 = (bf16[1,32,32,64]{3,2,1,0:T(8,128)(2,1)}, bf16[1,32,32,64]{3,2,1,0:T(8,128)(2,1)S(1)}, u32[]{:S(2)}) copy-start(bf16[1,32,32,64]{3,2,1,0:T(8,128)(2,1)S(1)} %collective-permute-done.2) | copy-start | bytes 393220
  47.0 1.5 copy-start.14
  67.0 10.8 %all-to-all-start = ((bf16[8,2,4096]{2,1,0:T(2,128)(2,1)}), bf16[8,2,4096]{2,1,0:T(2,128)(2,1)S(1)}, u32[]{:S(2)}, u32[]{:S(2)}) async-start(bf16[8,2,4096]{2,1,0:T(2,128)(2,1)} %reshape.223), calls=%async_computation | async-start | bytes 262144 | tf_op jit(solution)/shard_map/all_to_all | solution.py:94
  72.3 127.6 %reduce-scatter.2.cloned.1.call-start = ((), (), s32[]{:S(2)}) async-start(), calls=%async_computation.3 | async-start | bytes 4718592 | tf_op jit(solution)/shard_map/reduce_scatter | solution.py:99
  89.3 7.4 %copy-start.22 = (pred[8,3]{0,1:T(4,128)(4,1)S(1)}, pred[8,3]{0,1:T(4,128)(4,1)}, u32[]{:S(2)}) copy-start(pred[8,3]{0,1:T(4,128)(4,1)} %constant.62) | copy-start | bytes 76
  94.9 1.8 copy-start.8
  105.7 94.1 %copy-start.13 = (bf16[1,2,16,16,256]{4,3,2,1,0:T(8,128)(2,1)S(1)}, bf16[1,2,16,16,256]{4,3,2,1,0:T(8,128)(2,1)}, u32[]{:S(2)}) copy-start(bf16[1,2,16,16,256]{4,3,2,1,0:T(8,128)(2,1)} %param.9) | copy-start | bytes 786436
  105.8 148.5 %all-gather.2.cloned.1.call-start = ((), (), s32[]{:S(2)}) async-start(), calls=%async_computation.4 | async-start | bytes 2359296 | tf_op jit(solution)/shard_map/all_gather | solution.py:101
  202.0 2.8 copy-start.9
  287.0 44.2 %all-to-all-start.1 = ((bf16[8,2,4096]{2,1,0:T(2,128)(2,1)}), bf16[8,2,4096]{2,1,0:T(2,128)(2,1)S(1)}, u32[]{:S(2)}, u32[]{:S(2)}) async-start(bf16[8,2,4096]{2,1,0:T(2,128)(2,1)} %reshape.225), calls=%async_computation.2 | async-start | bytes 262144 | tf_op jit(solution)/shard_map/all_to_all | solution.py:105
  290.4 176.5 %all-reduce.7.cloned.1.call-start = ((), (), s32[]{:S(2)}) async-start(), calls=%async_computation.5 | async-start | bytes 442368 | tf_op jit(solution)/shard_map/psum | solution.py:106
  293.5 2.9 copy-start.2
  331.1 288.2 %all-reduce.9.cloned.1.call-start = ((), (), s32[]{:S(2)}) async-start(), calls=%async_computation.6 | async-start | bytes 1769472 | tf_op jit(solution)/shard_map/psum | solution.py:110
  337.2 1.6 copy-start.5
  340.6 1.8 copy-start.4
  362.6 258.9 %copy-start.1 = (bf16[3,3,3,128,256]{4,3,2,1,0:T(8,128)(2,1)S(1)}, bf16[3,3,3,128,256]{4,3,2,1,0:T(8,128)(2,1)}, u32[]{:S(2)}) copy-start(bf16[3,3,3,128,256]{4,3,2,1,0:T(8,128)(2,1)} %param.8) | copy-start | bytes 5308420
  (9 other events, 10.2 us)
Sparse Core Ops, SparseCore 0:
  105.9 93.9 reduce-scatter.1
  202.2 52.0 all-gather.1
  331.2 135.5 all-reduce.6
  472.8 146.4 all-reduce.8
where the time goes:
time: 638 us; the launch traced here: 628 us
  waiting for transfers between devices  410 us (64%)
  matrix products  99 us (16%)
  local copies, waits for them, and re-layouts  65.3 us (10%)
  starting transfers between devices  20.2 us (3%)
  other arithmetic  18.8 us (3%)
  between operations  14.7 us (2%)
    psum x1, waiting for transfers between devices, on_device(): lax.psum(kernel_grad(pad_sides(hidden), grad_mid), ('dp', 'space'))  151 us
    psum x1, waiting for transfers between devices, on_device(): lax.psum(deep_grad.astype(jnp.bfloat16), 'dp').astype(jnp.float32)  102 us
    reduce_scatter x1, waiting for transfers between devices, on_device(): lax.psum_scatter(partial_value, 'space', scatter_dimension=0, tiled=True)  93.6 us
    dot_general x54, matrix products, kernel_grad(): jnp.einsum('dhwi,dhwo->io', window, cotangent, preferred_element_type=jnp...  57.9 us
    all_gather x1, waiting for transfers between devices, on_device(): all_cotangent = lax.all_gather(grad_pre, 'space', axis=0, tiled=True)  46 us
    conv_general_dilated x4, matrix products, conv_depth(): lax.conv_general_dilated(padded[None], kernel, (1, 1, 1), [(0, 0), (1, 1)...  41.1 us
    unnamed x55, local copies, waits for them, and re-layouts  22.3 us
    conv_general_dilated x11, local copies, waits for them, and re-layouts, conv_depth(): lax.conv_general_dilated(padded[None], kernel, (1, 1, 1), [(0, 0), (1, 1)...  15.4 us
  transfers between devices with their start and end apart: 10, of which 8 were waited for; matrix products, arithmetic and copies ran while one was open for 12% of the time, Pallas kernels for 0%

commit v1 on v0

--- a/solution.py
+++ b/solution.py
@@ -107,7 +107,7 @@
     grad_mid = (expand(pooled_grad.astype(jnp.float32)) * 0.125 * activate_slope(pre_mid)).astype(
         jnp.bfloat16
     )
-    mid_grad = lax.psum(kernel_grad(pad_sides(hidden), grad_mid), ("dp", "space"))
+    mid_grad = lax.psum(lax.psum(kernel_grad(pad_sides(hidden), grad_mid), "dp"), "space")
     device_total = lax.axis_size("dp") * space_count
     cell_count = slab_depth * side_cells * side_cells
     deep_scale = math.sqrt(device_total * cell_count // 8)

time: 638 us -> 739 us (1.16)
  waiting for transfers between devices: 410 us -> 503 us
    psum x1 -> x2, waiting for transfers between devices: 151 us -> 208 us  [the longest x1 132 us: on_device(): lax.psum(kernel_grad(pad_sides(hidden), grad_mid), 'dp')]
    psum x1, waiting for transfers between devices: 102 us -> 137 us  [on_device(): lax.psum(deep_grad.astype(jnp.bfloat16), 'dp').astype(jnp.float32)]
    unnamed x55 -> x57, local copies, waits for them, and re-layouts: 22.3 us -> 22.3 us
  transfers between devices with their start and end apart: 10 -> 11, of which waited for: 8 -> 9; matrix products, arithmetic and copies ran while one was open for 12% -> 7% of each run, Pallas kernels for 0% -> 0%
where the time goes in v1:
time: 739 us; the launch traced here: 725 us
  waiting for transfers between devices  503 us (68%)
  matrix products  103 us (14%)
  local copies, waits for them, and re-layouts  65 us (9%)
  starting transfers between devices  20.3 us (3%)
  other arithmetic  18.7 us (3%)
  between operations  15 us (2%)
    psum x1, waiting for transfers between devices, on_device(): lax.psum(deep_grad.astype(jnp.bfloat16), 'dp').astype(jnp.float32)  137 us
    psum x1, waiting for transfers between devices, on_device(): lax.psum(kernel_grad(pad_sides(hidden), grad_mid), 'dp')  132 us
    reduce_scatter x1, waiting for transfers between devices, on_device(): lax.psum_scatter(partial_value, 'space', scatter_dimension=0, tiled=True)  93.8 us
    psum x1, waiting for transfers between devices, on_device(): lax.psum(lax.psum(kernel_grad(pad_sides(hidden), grad_mid), 'dp'), 'space')  76 us
    dot_general x54, matrix products, kernel_grad(): jnp.einsum('dhwi,dhwo->io', window, cotangent, preferred_element_type=jnp...  61.2 us
    all_gather x1, waiting for transfers between devices, on_device(): all_cotangent = lax.all_gather(grad_pre, 'space', axis=0, tiled=True)  46 us
    conv_general_dilated x4, matrix products, conv_depth(): lax.conv_general_dilated(padded[None], kernel, (1, 1, 1), [(0, 0), (1, 1)...  41.6 us
    unnamed x57, local copies, waits for them, and re-layouts  22.3 us
  transfers between devices with their start and end apart: 11, of which 9 were waited for; matrix products, arithmetic and copies ran while one was open for 7% of the time, Pallas kernels for 0%

profile of v1, /device:TPU:1, one launch (start us, length us, event | category | flops | bytes accessed | tf_op | source)
XLA Modules:
  0.0 725.3 jit_solution(10784802462196196043)
XLA Ops:
  8.2 4.0 collective-permute-start
  13.6 3.4 collective-permute-done.1
  18.2 7.4 %add_convert_fusion = (bf16[4,32,8,5,64]{4,2,3,1,0:T(8,128)(2,1)}, f32[4,32,8,5,64]{4,2,3,1,0:T(8,128)S(1)}, f32[4,32,8,5,64]{4,2,3,1,0:T(8,128)S(1)}, f32[4,32,8,5,64]{4,2,3,1,0:T(8,128)S(1)}) fusion(pred[8,5]{0,1:T(8,128)(4,1)S(1)} %copy-done.22, bf16[3,3,3,4,64]{4,3,2,1,0:T(4,128)(2,1)S(1)} %copy-done.21, bf16[6,32,1,7,2,4]{3,5,4,1,0,2:T(4,128)(2,1)S(1)} %slice.257, ...), kind=kOutput, calls=%fused_computation.31 | convolution fusion | flops 72511488 | bytes 4684328 | tf_op jit(solution)/shard_map/conv_general_dilated | solution.py:33
  27.5 4.7 fusion.30
  32.3 4.3 collective-permute-start.2
  39.8 7.1 collective-permute-done.3
  50.5 6.6 broadcast_multiply_fusion.1
  66.9 5.2 all-to-all-start
  72.2 5.5 all-to-all-done
  82.4 4.0 copy.321
  89.1 5.7 copy.215
  96.6 4.5 broadcast_select_fusion
  105.9 93.8 %reduce-scatter.2.cloned.1.call-done = f32[2,16,16,256]{3,1,2,0:T(8,128)} async-done(((f32[16,16,16,256]{3,1,2,0:T(8,128)}), f32[2,16,16,256]{3,1,2,0:T(8,128)}) %reduce-scatter.2.cloned.1.call-update) | async-done | bytes 524304 | tf_op jit(solution)/shard_map/reduce_scatter | solution.py:99
  208.2 46.0 %all-gather.2.cloned.1.call-done = bf16[16,16,16,256]{3,2,1,0:T(8,128)(2,1)} async-done(((bf16[2,16,16,256]{3,2,1,0:T(8,128)(2,1)}), bf16[16,16,16,256]{3,2,1,0:T(8,128)(2,1)}) %all-gather.2.cloned.1.call-update) | async-done | bytes 2097168 | tf_op jit(solution)/shard_map/all_gather | solution.py:101
  259.5 23.2 %select_convert_fusion = bf16[16,16,8,3,16]{4,2,3,1,0:T(8,128)(2,1)S(1)} fusion(pred[8,3]{0,1:T(4,128)(4,1)S(1)} %copy-done.23, bf16[18,16,1,7,2,256]{5,3,4,1,0,2:T(8,128)(2,1)S(1)} %slice.269, bf16[18,16,1,8,3,256]{5,3,4,1,0,2:T(8,128)(2,1)S(1)} %copy.221, bf16[3,3,3,128,256]{4,3,2,1,0:T(8,128)(2,1)S(1)} %copy-done, s32[]{:T(128)S(6)} %select_n.3), kind=kOutput, calls=%fused_computation.13 | convolution fusion | flops 1320222720 | bytes 6316548 | tf_op jit(solution)/shard_map/conv_general_dilated | solution.py:33
  284.3 3.1 reshape.225
  287.4 3.4 all-to-all-start.1
  291.2 3.0 fusion.179
  294.2 2.9 fusion.177
  358.5 3.0 fusion.133
  361.5 3.2 fusion.131
  368.1 132.0 %all-reduce.10.cloned.1.call-done = f32[3,3,3,64,128]{4,3,2,1,0:T(8,128)} async-done(((f32[3,3,3,64,128]{4,3,2,1,0:T(8,128)}), f32[3,3,3,64,128]{4,3,2,1,0:T(8,128)}) %all-reduce.10.cloned.1.call-update) | async-done | bytes 884752 | tf_op jit(solution)/shard_map/psum | solution.py:110
  500.9 137.5 %all-reduce.8.cloned.1.call-done = bf16[3,3,3,16,256]{4,3,2,1,0:T(8,128)(2,1)} async-done(((bf16[3,3,3,16,256]{4,3,2,1,0:T(8,128)(2,1)}), bf16[3,3,3,16,256]{4,3,2,1,0:T(8,128)(2,1)}) %all-reduce.8.cloned.1.call-update) | async-done | bytes 221200 | tf_op jit(solution)/shard_map/psum | solution.py:106
  640.1 76.0 %all-reduce.12.cloned.1.call-done = f32[3,3,3,64,128]{4,3,2,1,0:T(8,128)} async-done(((f32[3,3,3,64,128]{4,3,2,1,0:T(8,128)}), f32[3,3,3,64,128]{4,3,2,1,0:T(8,128)}) %all-reduce.12.cloned.1.call-update) | async-done | bytes 884752 | tf_op jit(solution)/shard_map/psum | solution.py:110
  (172 shorter events, 121.0 us)
Async XLA Ops:
  7.2 89.4 %copy-start = (bf16[3,3,3,128,256]{4,3,2,1,0:T(8,128)(2,1)S(1)}, bf16[3,3,3,128,256]{4,3,2,1,0:T(8,128)(2,1)}, u32[]{:S(2)}) copy-start(bf16[3,3,3,128,256]{4,3,2,1,0:T(8,128)(2,1)} %param.8) | copy-start | bytes 5308420
  7.2 11.0 %copy-start.22 = (pred[8,5]{0,1:T(8,128)(4,1)S(1)}, pred[8,5]{0,1:T(8,128)(4,1)}, u32[]{:S(2)}) copy-start(pred[8,5]{0,1:T(8,128)(4,1)} %constant.63) | copy-start | bytes 124
  7.2 11.0 %copy-start.21 = (bf16[3,3,3,4,64]{4,3,2,1,0:T(4,128)(2,1)S(1)}, bf16[3,3,3,4,64]{4,3,2,1,0:T(4,128)(2,1)}, u32[]{:S(2)}) copy-start(bf16[3,3,3,4,64]{4,3,2,1,0:T(4,128)(2,1)} %param.6) | copy-start | bytes 41476
  8.2 5.3 collective-permute-start
  12.3 4.7 collective-permute-start.1
  32.2 16.2 %copy-start.7 = (bf16[4,32,1,32,64]{4,3,1,2,0:T(8,128)(2,1)}, bf16[4,32,1,32,64]{4,3,1,2,0:T(8,128)(2,1)S(1)}, u32[]{:S(2)}) copy-start(bf16[4,32,1,32,64]{4,3,1,2,0:T(8,128)(2,1)S(1)} %fusion.30) | copy-start | bytes 1572868
  32.3 7.6 %collective-permute-start.2 = (bf16[1,32,32,64]{3,2,1,0:T(8,128)(2,1)S(1)}, bf16[1,32,32,64]{3,2,1,0:T(8,128)(2,1)S(1)}, u32[]{:S(2)}, u32[]{:S(2)}) collective-permute-start(bf16[1,32,32,64]{3,2,1,0:T(8,128)(2,1)S(1)} %get-tuple-element.18), channel_id=1, source_target_pairs={{0,1},{1,2},{2,3},{3,4},{4,5},{5,6},{6,7},{8,9},{9,10},{10,11},{11... | collective-permute-start | bytes 393224 | tf_op jit(solution)/shard_map/ppermute | solution.py:15
  36.6 10.3 %collective-permute-start.3 = (bf16[1,32,32,64]{3,2,1,0:T(8,128)(2,1)S(1)}, bf16[1,32,32,64]{3,2,1,0:T(8,128)(2,1)S(1)}, u32[]{:S(2)}, u32[]{:S(2)}) collective-permute-start(bf16[1,32,32,64]{3,2,1,0:T(8,128)(2,1)S(1)} %get-tuple-element.19), channel_id=1, source_target_pairs={{1,0},{2,1},{3,2},{4,3},{5,4},{6,5},{7,6},{9,8},{10,9},{11,10},{12... | collective-permute-start | bytes 393224 | tf_op jit(solution)/shard_map/ppermute | solution.py:18
  39.8 8.6 %copy-start.17 = (bf16[1,32,32,64]{3,2,1,0:T(8,128)(2,1)}, bf16[1,32,32,64]{3,2,1,0:T(8,128)(2,1)S(1)}, u32[]{:S(2)}) copy-start(bf16[1,32,32,64]{3,2,1,0:T(8,128)(2,1)S(1)} %collective-permute-done.2) | copy-start | bytes 393220
  66.9 10.8 %all-to-all-start = ((bf16[8,2,4096]{2,1,0:T(2,128)(2,1)}), bf16[8,2,4096]{2,1,0:T(2,128)(2,1)S(1)}, u32[]{:S(2)}, u32[]{:S(2)}) async-start(bf16[8,2,4096]{2,1,0:T(2,128)(2,1)} %reshape.223), calls=%async_computation | async-start | bytes 262144 | tf_op jit(solution)/shard_map/all_to_all | solution.py:94
  72.1 127.6 %reduce-scatter.2.cloned.1.call-start = ((), (), s32[]{:S(2)}) async-start(), calls=%async_computation.3 | async-start | bytes 4718592 | tf_op jit(solution)/shard_map/reduce_scatter | solution.py:99
  89.1 7.4 %copy-start.23 = (pred[8,3]{0,1:T(4,128)(4,1)S(1)}, pred[8,3]{0,1:T(4,128)(4,1)}, u32[]{:S(2)}) copy-start(pred[8,3]{0,1:T(4,128)(4,1)} %constant.62) | copy-start | bytes 76
  94.8 1.8 copy-start.9
  105.6 94.1 %copy-start.14 = (bf16[1,2,16,16,256]{4,3,2,1,0:T(8,128)(2,1)S(1)}, bf16[1,2,16,16,256]{4,3,2,1,0:T(8,128)(2,1)}, u32[]{:S(2)}) copy-start(bf16[1,2,16,16,256]{4,3,2,1,0:T(8,128)(2,1)} %param.9) | copy-start | bytes 786436
  105.6 148.6 %all-gather.2.cloned.1.call-start = ((), (), s32[]{:S(2)}) async-start(), calls=%async_computation.4 | async-start | bytes 2359296 | tf_op jit(solution)/shard_map/all_gather | solution.py:101
  201.9 2.8 copy-start.10
  287.4 38.1 %all-to-all-start.1 = ((bf16[8,2,4096]{2,1,0:T(2,128)(2,1)}), bf16[8,2,4096]{2,1,0:T(2,128)(2,1)S(1)}, u32[]{:S(2)}, u32[]{:S(2)}) async-start(bf16[8,2,4096]{2,1,0:T(2,128)(2,1)} %reshape.225), calls=%async_computation.2 | async-start | bytes 262144 | tf_op jit(solution)/shard_map/all_to_all | solution.py:105
  290.7 209.3 %all-reduce.10.cloned.1.call-start = ((), (), s32[]{:S(2)}) async-start(), calls=%async_computation.6 | async-start | bytes 1769472 | tf_op jit(solution)/shard_map/psum | solution.py:110
  294.2 2.9 copy-start.2
  334.7 1.7 copy-start.5
  358.4 279.9 %all-reduce.8.cloned.1.call-start = ((), (), s32[]{:S(2)}) async-start(), calls=%async_computation.5 | async-start | bytes 442368 | tf_op jit(solution)/shard_map/psum | solution.py:106
  361.5 3.2 copy-start.3
  365.9 352.4 %copy-start.1 = (bf16[3,3,3,128,256]{4,3,2,1,0:T(8,128)(2,1)S(1)}, bf16[3,3,3,128,256]{4,3,2,1,0:T(8,128)(2,1)}, u32[]{:S(2)}) copy-start(bf16[3,3,3,128,256]{4,3,2,1,0:T(8,128)(2,1)} %param.8) | copy-start | bytes 5308420
  368.0 348.1 %all-reduce.12.cloned.1.call-start = ((), (), s32[]{:S(2)}) async-start(), calls=%async_computation.7 | async-start | bytes 1769472 | tf_op jit(solution)/shard_map/psum | solution.py:110
  (11 other events, 13.3 us)
Sparse Core Ops, SparseCore 0:
  105.7 93.9 reduce-scatter.1
  202.0 52.1 all-gather.1
  358.6 141.4 all-reduce.9
  503.1 135.1 all-reduce.7
  640.7 75.3 all-reduce.11
